TPU v7x, 32 devices: a whole 2x2x4 slice. The times are simulated.
32 devices in a mesh: cells: 2 (over x), tp: 16 (over z, y, core).
Axes of the slice: x: 2, y: 2, z: 4, core: 2. Of those that a mesh axis runs over, the one named last changes fastest.
Arguments:
- hidden: bfloat16 [64, 8192], P(('cells', 'tp')), parts along dimension 0, may hold values from -6 to 6
- norm_gain: bfloat16 [8192], replicated, may hold values from 0.099609375 to 1.8984375
- qkv_weight: bfloat16 [8192, 10240], P(None, 'tp'), may hold values from -0.0625 to 0.0625
- out_weight: bfloat16 [8192, 8192], P('tp'), may hold values from -0.0625 to 0.0625
- key_values: bfloat16 [64, 64, 2048], P(('cells', 'tp')), parts along dimension 0, may hold values from -260 to 260
- cache_lengths: int32 [64], P(('cells', 'tp')), parts along dimension 0, may hold values from 1 to 64, as said below
- adapter_ids: int32 [2, 64], P(None, 'cells'), parts along dimension 1, may hold values from 0 to 63
- page_table: int32 [128, 16], P('cells'), parts along dimension 0, may hold values from 0 to 1023, as said below
- down_pages: bfloat16 [1024, 512, 256], P('tp'), may hold values from -0.0625 to 0.0625
- up_pages: bfloat16 [1024, 64, 1152], P('tp'), may hold values from -0.75 to 0.75
Outputs:
- final_hidden: bfloat16 [64, 8192], P(('cells', 'tp')), parts along dimension 0
There are 2 independent parts, one for each index of `cells`. A program takes and returns all parts, laid end to end along the dimension named above; an argument that names none is the same for every part. Nothing has to cross between parts.
Inputs may be any that keep to these rules, and one draw needn't show every extreme that they name: page_table[a, p] // 64 is the index along tp of the device that holds page p of adapter a. Every slot holds one page, and every device holds exactly one page of each adapter. For each pair of devices, at most 8 adapters have their page for the second device held on the first, and some pair reaches 8. `cache_lengths`: some request has a full cache.
All inputs are finite; a program needn't handle non-finite values.
Results may differ from a plain program's by a relative error of at most 0.024.
Values may be sent and summed in bfloat16 or wider, within the bound.
No kernel may reach another device: no remote copies, remote signals or barrier semaphores. Data moves between devices by JAX's collectives and lax.ppermute only.
A program may use at most 384 MiB of HBM per device.

v0:
```python
import jax
import jax.numpy as jnp
from jax import lax
from jax.sharding import PartitionSpec as P

HEADS = 64
KVH = 8
HD = 128
RANK = 64
STEPS = 2


rope_base = 500000.0
norm_eps = 1e-05


def rotate(values, position):
    half_dim = values.shape[-1] // 2
    frequency = rope_base ** (-(jnp.arange(half_dim, dtype=jnp.float32) * 2.0) / values.shape[-1])
    angles = position.astype(jnp.float32)[:, None] * frequency[None, :]
    cosine = jnp.cos(angles)[:, None, :]
    sine_part = jnp.sin(angles)[:, None, :]
    leading = values[..., :half_dim]
    second = values[..., half_dim:]
    return jnp.concatenate(
        [leading * cosine - second * sine_part, second * cosine + leading * sine_part], axis=-1
    )


def attend(queries, cached, lengths, fresh_keys, fresh_values):
    row_count = queries.shape[0]
    positions = cached.shape[1]
    keys_old = cached[:, :, : KVH * HD].reshape(row_count, positions, KVH, HD)
    values_old = cached[:, :, KVH * HD :].reshape(row_count, positions, KVH, HD)
    scaling = HD ** (-0.5)
    old_scores = (
        jnp.einsum("rgqd,rjgd->rgqj", queries, keys_old, preferred_element_type=jnp.float32)
        * scaling
    )
    visible = jnp.arange(positions, dtype=jnp.int32)[None, :] < lengths[:, None]
    old_scores = jnp.where(visible[:, None, None, :], old_scores, -jnp.inf)
    new_scores = (
        jnp.einsum("rgqd,rugd->rgqu", queries, fresh_keys, preferred_element_type=jnp.float32)
        * scaling
    )
    scores = jnp.concatenate([old_scores, new_scores], axis=-1)
    highest = jnp.max(scores, axis=-1, keepdims=True)
    exps = jnp.exp(scores - highest)
    weights = (exps / jnp.sum(exps, axis=-1, keepdims=True)).astype(jnp.bfloat16)
    mixed = jnp.einsum(
        "rgqj,rjgd->rgqd", weights[..., :positions], values_old, preferred_element_type=jnp.float32
    )
    mixed = mixed + jnp.einsum(
        "rgqu,rugd->rgqd",
        weights[..., positions:],
        fresh_values,
        preferred_element_type=jnp.float32,
    )
    return mixed.reshape(row_count, HEADS * HD).astype(jnp.bfloat16)


def body(
    hidden,
    norm_gain,
    qkv_weight,
    out_weight,
    key_values,
    cache_lengths,
    adapter_ids,
    page_table,
    down_pages,
    up_pages,
):
    shards = lax.axis_size("tp")
    my_index = lax.axis_index("tp")
    rows_dev = hidden.shape[0]
    width = hidden.shape[1]
    qkv_slice = qkv_weight.shape[1]
    slice_width = out_weight.shape[0]
    adapters = page_table.shape[0]
    kv_width = KVH * HD
    capacity = max(2, 2 * adapters // shards)
    owner_dev = page_table // adapters
    local_slot = page_table % adapters
    adapter_iota = jnp.arange(adapters, dtype=jnp.int32)
    device_iota = jnp.arange(shards, dtype=jnp.int32)
    earlier = adapter_iota[None, :, None] < adapter_iota[:, None, None]
    shared = (owner_dev[None, :, :] == owner_dev[:, None, :]) & earlier
    rank_among = jnp.sum(shared.astype(jnp.int32), axis=1)
    held_here = (owner_dev == my_index).astype(jnp.int32)
    target = jnp.sum(held_here * device_iota[None, :], axis=1)
    held_slot = jnp.sum(held_here * local_slot, axis=1)
    send_row = target * capacity + jnp.sum(held_here * rank_among, axis=1)
    source = lax.dynamic_slice_in_dim(owner_dev, my_index, 1, 1)[:, 0]
    arrival_rank = lax.dynamic_slice_in_dim(rank_among, my_index, 1, 1)[:, 0]
    recv_row = source * capacity + arrival_rank

    def outgoing(pages):
        ordered = jnp.take(pages, held_slot, axis=0)
        zeroed = jnp.zeros((shards * capacity,) + pages.shape[1:], pages.dtype)
        return zeroed.at[send_row].set(ordered)

    arrived_down, arrived_up = (
        lax.all_to_all(outgoing(down_pages), "tp", split_axis=0, concat_axis=0, tiled=True),
        lax.all_to_all(outgoing(up_pages), "tp", split_axis=0, concat_axis=0, tiled=True),
    )
    need_down = jnp.take(arrived_down, recv_row, axis=0)
    need_up = jnp.take(arrived_up, recv_row, axis=0)
    need_out = need_down[:, :, 3 * RANK :]
    qkv_down = need_down[:, :, : 3 * RANK]
    up_qkv_part = need_up[:, :, :qkv_slice]
    up_out_part = need_up[:, :, qkv_slice:]
    columns = my_index * qkv_slice + jnp.arange(qkv_slice, dtype=jnp.int32)
    key_limit = width + kv_width
    residual = hidden
    keys_kept = []
    values_kept = []
    for decode_step in range(STEPS):
        chosen_all = adapter_ids[decode_step]
        widened = residual.astype(jnp.float32)
        normed = (
            widened
            * lax.rsqrt(jnp.mean(widened * widened, axis=1, keepdims=True) + norm_eps)
            * norm_gain.astype(jnp.float32)
        ).astype(jnp.bfloat16)
        project_portion = lax.all_gather(normed, "tp", axis=0, tiled=True)
        projected = jnp.dot(project_portion, qkv_weight, preferred_element_type=jnp.float32)
        picked = lax.dynamic_slice_in_dim(project_portion, my_index * slice_width, slice_width, 1)
        joined = jnp.concatenate(
            [
                projected,
                jnp.einsum(
                    "rd,rdk->rk",
                    picked,
                    jnp.take(qkv_down, chosen_all, axis=0),
                    preferred_element_type=jnp.float32,
                ),
            ],
            axis=1,
        )
        projected = joined[:, :qkv_slice]
        shrink = lax.psum(joined[:, qkv_slice:], "tp").astype(jnp.bfloat16)
        up_rows = jnp.take(up_qkv_part, chosen_all, axis=0)
        query_terms = jnp.einsum(
            "rk,rkc->rc", shrink[:, :RANK], up_rows, preferred_element_type=jnp.float32
        )
        key_terms = jnp.einsum(
            "rk,rkc->rc", shrink[:, RANK : 2 * RANK], up_rows, preferred_element_type=jnp.float32
        )
        value_terms = jnp.einsum(
            "rk,rkc->rc", shrink[:, 2 * RANK :], up_rows, preferred_element_type=jnp.float32
        )
        adapter_terms = jnp.where(
            columns[None, :] < width,
            query_terms,
            jnp.where(columns[None, :] < key_limit, key_terms, value_terms),
        )
        joint = (projected + adapter_terms).astype(jnp.bfloat16)
        row_joint = lax.all_to_all(joint, "tp", split_axis=0, concat_axis=1, tiled=True)
        position = cache_lengths + decode_step
        queries = rotate(
            row_joint[:, :width].astype(jnp.float32).reshape(rows_dev, HEADS, HD), position
        ).astype(jnp.bfloat16)
        key_now = rotate(
            row_joint[:, width:key_limit].astype(jnp.float32).reshape(rows_dev, KVH, HD), position
        ).astype(jnp.bfloat16)
        keys_kept.append(key_now)
        values_kept.append(row_joint[:, key_limit:].reshape(rows_dev, KVH, HD))
        attn = attend(
            queries.reshape(rows_dev, KVH, HEADS // KVH, HD),
            key_values,
            cache_lengths,
            jnp.stack(keys_kept, axis=1),
            jnp.stack(values_kept, axis=1),
        )
        headwise = lax.all_to_all(attn, "tp", split_axis=1, concat_axis=0, tiled=True)
        out_partial = jnp.einsum(
            "rd,rdk->rk",
            headwise,
            jnp.take(need_out, chosen_all, axis=0),
            preferred_element_type=jnp.float32,
        )
        out_shrink = lax.psum(out_partial, "tp").astype(jnp.bfloat16)
        out_terms = jnp.einsum(
            "rk,rkc->rc",
            out_shrink,
            jnp.take(up_out_part, chosen_all, axis=0),
            preferred_element_type=jnp.float32,
        )
        summed = lax.psum_scatter(
            jnp.dot(headwise, out_weight, preferred_element_type=jnp.float32),
            "tp",
            scatter_dimension=0,
            tiled=True,
        )
        summed = summed + lax.all_to_all(out_terms, "tp", split_axis=0, concat_axis=1, tiled=True)
        residual = (residual.astype(jnp.float32) + summed).astype(jnp.bfloat16)
    return residual


def solution(mesh):
    in_specs = (
        P(("cells", "tp"), None),
        P(),
        P(None, "tp"),
        P("tp", None),
        P(("cells", "tp"), None, None),
        P(("cells", "tp")),
        P(None, "cells"),
        P("cells", None),
        P("tp", None, None),
        P("tp", None, None),
    )
    out_specs = P(("cells", "tp"), None)
    return jax.shard_map(body, mesh=mesh, in_specs=in_specs, out_specs=out_specs, check_vma=False)
```

profile of v0, /device:TPU:0, one launch (start us, length us, event | category | flops | bytes accessed | tf_op | source)
XLA Modules:
  0.0 1725.1 jit_solution(6231995954266456240)
XLA Ops:
  9.4 10.0 gather_fusion.2
  19.4 8.5 broadcast_select_fusion.2
  27.9 7.3 broadcast_in_dim.161
  35.2 23.4 %scatter_fusion.1 = bf16[128,64,1152]{2,1,0:T(8,128)(2,1)} fusion(bf16[128,64,1152]{2,1,0:T(8,128)(2,1)} %broadcast_in_dim.161, s32[64]{0:T(128)S(1)} %fusion.59, bf16[64,64,1152]{2,1,0:T(8,128)(2,1)} %broadcast_select_fusion.2), kind=kCustom, calls=%fused_computation.13 | custom fusion | bytes 28311808 | tf_op jit(solution)/shard_map/scatter | solution.py:101
  58.6 7.5 all-to-all-start.1
  66.1 13.6 gather_fusion
  79.7 14.2 broadcast_select_fusion
  93.9 10.8 broadcast_in_dim.157
  104.8 42.3 %scatter_fusion = bf16[128,512,256]{2,1,0:T(8,128)(2,1)} fusion(bf16[128,512,256]{2,1,0:T(8,128)(2,1)} %broadcast_in_dim.157, s32[64]{0:T(128)S(1)} %fusion.59, bf16[64,512,256]{2,1,0:T(8,128)(2,1)} %broadcast_select_fusion), kind=kCustom, calls=%fused_computation.12 | custom fusion | bytes 50331904 | tf_op jit(solution)/shard_map/scatter | solution.py:101
  147.1 252.3 %all-to-all-done.1 = bf16[128,64,1152]{2,1,0:T(8,128)(2,1)} async-done(((bf16[128,64,1152]{2,1,0:T(8,128)(2,1)}), bf16[128,64,1152]{2,1,0:T(8,128)(2,1)}, u32[]{:S(2)}, u32[]{:S(2)}) %all-to-all-start.1) | async-done | bytes 18874400 | tf_op jit(solution)/shard_map/all_to_all | solution.py:105
  399.4 78.7 %all-to-all-start = ((bf16[128,512,256]{2,1,0:T(8,128)(2,1)}), bf16[128,512,256]{2,1,0:T(8,128)(2,1)}, u32[]{:S(2)}, u32[]{:S(2)}) async-start(bf16[128,512,256]{2,1,0:T(8,128)(2,1)} %scatter_fusion), calls=%async_computation | async-start | bytes 67108864 | tf_op jit(solution)/shard_map/all_to_all | solution.py:104
  478.4 639.4 %all-gather = bf16[16,2,8192]{2,1,0:T(2,128)(2,1)S(1)} all-gather(bf16[1,2,8192]{2,1,0:T(2,128)(2,1)S(1)} %fusion.65), channel_id=1, replica_groups=mesh['cells'=2,'tp'=16] {'tp'}, dimensions={0}, use_global_device_ids=true | all-gather | bytes 557056 | tf_op jit(solution)/shard_map/all_gather | solution.py:126
  1120.0 12.6 gather_fusion.3
  1132.6 8.3 broadcast_select_fusion.3
  1140.9 5.3 slice.156
  1146.2 3.5 gather_fusion.5
  1149.7 11.8 gather_fusion.1
  1161.6 14.2 broadcast_select_fusion.1
  1175.7 10.8 gather_fusion.4
  1186.5 4.7 fusion.2
  1191.2 154.6 %psum.28 = bf16[32,192]{1,0:T(8,128)(2,1)S(1)} all-reduce(f32[32,192]{1,0:T(8,128)S(1)} %bitcast.180), channel_id=1, replica_groups=mesh['cells'=2,'tp'=16] {'tp'}, use_global_device_ids=true, to_apply=%region_6.8 | all-reduce | flops 6144 | bytes 36864 | tf_op jit(solution)/shard_map/psum | solution.py:142
  1347.7 5.7 fusion.24
  1354.1 3.5 all-to-all-start.2
  1357.6 6.6 all-to-all-done.2
  1366.7 3.5 all-to-all-start.3
  1370.5 4.7 slice.169
  1378.0 9.0 slice.168
  1387.1 6.5 gather_fusion.6
  1393.6 5.9 fusion.118
  1399.5 2.9 fusion.8
  1402.5 62.4 %psum.29 = bf16[32,64]{1,0:T(8,128)(2,1)S(1)} all-reduce(f32[32,64]{1,0:T(8,128)S(1)} %bitcast.186), channel_id=1, replica_groups=mesh['cells'=2,'tp'=16] {'tp'}, use_global_device_ids=true, to_apply=%region_11.15 | all-reduce | flops 2048 | bytes 12288 | tf_op jit(solution)/shard_map/psum | solution.py:183
  1466.0 3.5 all-to-all-start.4
  1470.8 3.6 gather_fusion.9
  1474.4 10.8 gather_fusion.8
  1485.2 9.4 all-reduce.5.cloned.1.call-done
  1495.9 22.4 %all-gather.1 = bf16[16,2,8192]{2,1,0:T(2,128)(2,1)} all-gather(bf16[1,2,8192]{2,1,0:T(2,128)(2,1)S(1)} %fusion.64), channel_id=1, replica_groups=mesh['cells'=2,'tp'=16] {'tp'}, dimensions={0}, use_global_device_ids=true | all-gather | bytes 557056 | tf_op jit(solution)/shard_map/all_gather | solution.py:126
  1519.6 4.7 fusion
  1524.3 57.9 %psum.30 = bf16[32,192]{1,0:T(8,128)(2,1)S(1)} all-reduce(f32[32,192]{1,0:T(8,128)S(1)} %bitcast.181), channel_id=1, replica_groups=mesh['cells'=2,'tp'=16] {'tp'}, use_global_device_ids=true, to_apply=%region_13.18 | all-reduce | flops 6144 | bytes 36864 | tf_op jit(solution)/shard_map/psum | solution.py:142
  1584.1 5.7 fusion.25
  1590.5 3.5 all-to-all-start.5
  1594.0 6.6 all-to-all-done.5
  1603.0 3.5 all-to-all-start.6
  1609.5 6.4 gather_fusion.10
  1616.0 6.0 fusion.119
  1621.9 2.9 fusion.6
  1624.9 62.4 %psum.31 = bf16[32,64]{1,0:T(8,128)(2,1)S(1)} all-reduce(f32[32,64]{1,0:T(8,128)S(1)} %bitcast.187), channel_id=1, replica_groups=mesh['cells'=2,'tp'=16] {'tp'}, use_global_device_ids=true, to_apply=%region_18.23 | all-reduce | flops 2048 | bytes 12288 | tf_op jit(solution)/shard_map/psum | solution.py:183
  1687.8 9.5 all_to_all.118
  1697.2 19.4 %all-reduce.7.cloned.1.call-done = f32[32,8192]{1,0:T(8,128)} async-done(((f32[32,8192]{1,0:T(8,128)}), f32[32,8192]{1,0:T(8,128)}) %all-reduce.7.cloned.1.call-update) | async-done | bytes 1048592
  (135 shorter events, 27.6 us)
Async XLA Ops:
  58.6 340.8 %all-to-all-start.1 = ((bf16[128,64,1152]{2,1,0:T(8,128)(2,1)}), bf16[128,64,1152]{2,1,0:T(8,128)(2,1)}, u32[]{:S(2)}, u32[]{:S(2)}) async-start(bf16[128,64,1152]{2,1,0:T(8,128)(2,1)} %scatter_fusion.1), calls=%async_computation.1 | async-start | bytes 37748736 | tf_op jit(solution)/shard_map/all_to_all | solution.py:105
  147.1 331.0 %copy-start.4 = (bf16[8192]{0:T(1024)(128)(2,1)S(1)}, bf16[8192]{0:T(1024)(128)(2,1)}, u32[]{:S(2)}) copy-start(bf16[8192]{0:T(1024)(128)(2,1)} %param.19) | copy-start | bytes 49156
  147.1 331.0 %copy-start.3 = (bf16[2,8192]{1,0:T(2,128)(2,1)S(1)}, bf16[2,8192]{1,0:T(2,128)(2,1)}, u32[]{:S(2)}) copy-start(bf16[2,8192]{1,0:T(2,128)(2,1)} %param.18) | copy-start | bytes 98308
  147.1 971.4 %copy-start.6 = (s32[2,32]{1,0:T(2,128)S(1)}, s32[2,32]{1,0:T(2,128)}, u32[]{:S(2)}) copy-start(s32[2,32]{1,0:T(2,128)} %param.24) | copy-start | bytes 772
  147.1 972.0 %copy-start.10 = (s32[2]{0:T(128)S(1)}, s32[2]{0:T(128)}, u32[]{:S(2)}) copy-start(s32[2]{0:T(128)} %param.23) | copy-start | bytes 28
  147.1 972.1 %copy-start.2 = (bf16[2,64,2048]{2,1,0:T(8,128)(2,1)S(1)}, bf16[2,64,2048]{2,1,0:T(8,128)(2,1)}, u32[]{:S(2)}) copy-start(bf16[2,64,2048]{2,1,0:T(8,128)(2,1)} %param.22) | copy-start | bytes 1572868
  399.4 750.3 %all-to-all-start = ((bf16[128,512,256]{2,1,0:T(8,128)(2,1)}), bf16[128,512,256]{2,1,0:T(8,128)(2,1)}, u32[]{:S(2)}, u32[]{:S(2)}) async-start(bf16[128,512,256]{2,1,0:T(8,128)(2,1)} %scatter_fusion), calls=%async_computation | async-start | bytes 67108864 | tf_op jit(solution)/shard_map/all_to_all | solution.py:104
  1119.1 228.0 %copy-start.8 = (pred[32]{0:T(512)(128)(4,1)}, pred[32]{0:T(512)(128)(4,1)S(1)}, u32[]{:S(2)}) copy-start(pred[32]{0:T(512)(128)(4,1)S(1)} %get-tuple-element.45) | copy-start | bytes 100
  1347.7 9.9 copy-start.11
  1347.7 18.1 %copy-start = (bf16[2,8,8,8,128]{4,3,2,1,0:T(8,128)(2,1)S(1)}, bf16[2,8,8,8,128]{4,3,2,1,0:T(8,128)(2,1)}, u32[]{:S(2)}) copy-start(bf16[2,8,8,8,128]{4,3,2,1,0:T(8,128)(2,1)} %get-tuple-element.21) | copy-start | bytes 786436
  1354.1 10.1 all-to-all-start.2
  1366.7 26.9 %all-to-all-start.3 = ((bf16[2,16,512]{2,0,1:T(2,128)(2,1)}), bf16[2,16,512]{2,0,1:T(2,128)(2,1)S(1)}, u32[]{:S(2)}, u32[]{:S(2)}) async-start(bf16[2,16,512]{2,0,1:T(2,128)(2,1)} %copy.107), calls=%async_computation.3 | async-start | bytes 65536 | tf_op jit(solution)/shard_map/all_to_all | solution.py:176
  1370.2 124.4 %all-reduce.5.cloned.1.call-start = ((), (), s32[]{:S(2)}) async-start(), calls=%async_computation.8 | async-start | bytes 2097152
  1393.6 6.0 copy-start.9
  1399.5 70.0 %copy-start.12 = (u32[32]{0:T(128)S(1)}, u32[32]{0:T(128)}, u32[]{:S(2)}) copy-start(u32[32]{0:T(128)} %constant.172) | copy-start | bytes 388
  1399.5 71.2 %copy-start.5 = (s32[32]{0:T(128)S(1)}, s32[32]{0:T(128)}, u32[]{:S(2)}) copy-start(s32[32]{0:T(128)} %get-tuple-element.15) | copy-start | bytes 388
  1466.0 19.2 %all-to-all-start.4 = ((f32[16,2,512]{2,1,0:T(2,128)}), f32[16,2,512]{2,1,0:T(2,128)S(1)}, u32[]{:S(2)}, u32[]{:S(2)}) async-start(f32[16,2,512]{2,1,0:T(2,128)} %all_to_all.95), calls=%async_computation.4 | async-start | bytes 131072 | tf_op jit(solution)/shard_map/all_to_all | solution.py:196
  1474.4 45.2 %copy-start.7 = (pred[32]{0:T(512)(128)(4,1)S(1)}, pred[32]{0:T(512)(128)(4,1)}, u32[]{:S(2)}) copy-start(pred[32]{0:T(512)(128)(4,1)} %get-tuple-element.14) | copy-start | bytes 100
  1584.1 17.8 %copy-start.1 = (bf16[2,8,8,8,128]{4,3,2,1,0:T(8,128)(2,1)S(1)}, bf16[2,8,8,8,128]{4,3,2,1,0:T(8,128)(2,1)}, u32[]{:S(2)}) copy-start(bf16[2,8,8,8,128]{4,3,2,1,0:T(8,128)(2,1)} %get-tuple-element.21) | copy-start | bytes 786436
  1590.5 10.2 all-to-all-start.5
  1603.0 12.9 all-to-all-start.6
  1606.5 110.2 %all-reduce.7.cloned.1.call-start = ((), (), s32[]{:S(2)}) async-start(), calls=%async_computation.9 | async-start | bytes 2097152
Sparse Core Ops, SparseCore 0:
  1399.6 94.9 all-reduce.4
  1622.1 94.5 all-reduce.6
where the time goes:
time: 1730 us
  blocking collectives  1010 us (58%)
  waiting for transfers between devices  294 us (17%)
  local copies, waits for them, and re-layouts  206 us (12%)
  starting transfers between devices  104 us (6%)
  other arithmetic  52.7 us (3%)
  matrix products  45 us (3%)
    all_gather x2, blocking collectives, body(): project_portion = lax.all_gather(normed, 'tp', axis=0, tiled=True)  662 us
    all_to_all x1, waiting for transfers between devices, body(): lax.all_to_all(outgoing(up_pages), 'tp', split_axis=0, concat_axis=0, til...  252 us
    psum x2, blocking collectives, body(): shrink = lax.psum(joined[:, qkv_slice:], 'tp').astype(jnp.bfloat16)  212 us
    psum x2, blocking collectives, body(): out_shrink = lax.psum(out_partial, 'tp').astype(jnp.bfloat16)  125 us
    all_to_all x1, starting transfers between devices, body(): lax.all_to_all(outgoing(down_pages), 'tp', split_axis=0, concat_axis=0, t...  78.7 us
    scatter x2, local copies, waits for them, and re-layouts, outgoing(): return zeroed.at[send_row].set(ordered)  65.7 us
  transfers between devices with their start and end apart: 9, of which 5 were waited for; matrix products, arithmetic and copies ran while one was open for 10% of the time, Pallas kernels for 0%

commit v1 on v0

v1 whole, which is shorter than its diff:
```python
import functools

import jax
import jax.numpy as jnp
from jax import lax
from jax.experimental import pallas as pl
from jax.experimental.pallas import tpu as pltpu
from jax.sharding import PartitionSpec as P

HEADS = 64
KVH = 8
HD = 128
RANK = 64
STEPS = 2
LANES = 128
CHUNK = 4
SPAN = 512
VMEM_LIMIT = 48 * 1024 * 1024

rope_base = 500000.0
norm_eps = 1e-05
BF16 = jnp.bfloat16
F32 = jnp.float32


def lane_window(first, width, total):
    if total % LANES:
        return 0, total
    low = first // LANES * LANES
    high = -(-(first + width) // LANES) * LANES
    return low, high - low


class Pages:
    def __init__(self, count, slots, pool, buffer, sems, first):
        self.chunks = (count[0] + CHUNK - 1) // CHUNK
        self.slots, self.pool, self.buffer, self.sems = slots, pool, buffer, sems
        self.first = first

    def start(self):
        width = self.buffer.shape[2]

        def begin(chunk, carry):
            for inner in range(CHUNK):
                at = chunk * CHUNK + inner
                pltpu.make_async_copy(
                    self.pool.at[self.slots[at], :, pl.ds(self.first, width)],
                    self.buffer.at[at],
                    self.sems.at[chunk],
                ).start()
            return carry

        lax.fori_loop(0, self.chunks, begin, 0)

    def each(self, step):
        def run(chunk, carry):
            base = pl.multiple_of(chunk * CHUNK, CHUNK)
            group = self.buffer.at[pl.ds(base, CHUNK)]
            pltpu.make_async_copy(group, group, self.sems.at[chunk]).wait()
            for inner in range(CHUNK):
                step(base + inner)
            return carry

        lax.fori_loop(0, self.chunks, run, 0)


def on_pages(kernel, out_shape, scalars, arrays, pool, window, name, scratch=()):
    used = scalars[1].shape[0]
    shape = (used, pool.shape[1], window[1])
    return pl.pallas_call(
        kernel,
        out_shape=out_shape,
        in_specs=[pl.BlockSpec(memory_space=pltpu.SMEM)] * len(scalars)
        + [pl.BlockSpec(memory_space=pltpu.VMEM)] * len(arrays)
        + [pl.BlockSpec(memory_space=pltpu.HBM)],
        out_specs=jax.tree.map(lambda _: pl.BlockSpec(memory_space=pltpu.VMEM), out_shape),
        scratch_shapes=[
            pltpu.VMEM(shape, pool.dtype),
            pltpu.SemaphoreType.DMA((used // CHUNK,)),
            *scratch,
        ],
        compiler_params=pltpu.CompilerParams(vmem_limit_bytes=VMEM_LIMIT),
        cost_estimate=pl.CostEstimate(
            flops=0,
            bytes_accessed=2 * used * shape[1] * shape[2],
            transcendentals=0,
        ),
        name=name,
    )(*scalars, *arrays, pool)


def put(total, columns, place, at, found, add=False):
    wanted = place == at
    for low in range(0, found.shape[1], LANES):
        wide = min(LANES, found.shape[1] - low)
        window = (slice(None), pl.ds(pl.multiple_of(columns + low, wide), wide))
        old = total[window]
        new = found[:, low : low + wide]
        total[window] = jnp.where(wanted[:, :wide], old + new if add else new, old)


def normalise(state, into, gain, normed):
    rows, width = state.shape
    squares = jnp.zeros((rows, SPAN), F32)
    for low in range(0, width, SPAN):
        widened = state[:, low : low + SPAN].astype(F32)
        squares = squares + widened * widened
    mean = jnp.sum(squares, axis=1, keepdims=True) / width
    scale = lax.rsqrt(mean + norm_eps)
    for low in range(0, width, SPAN):
        widened = state[:, low : low + SPAN].astype(F32)
        rounded = widened * scale * gain[:, low : low + SPAN].astype(F32)
        normed[into, low : low + SPAN] = rounded.astype(BF16)


def shrink_pages(pages, blocks, place, normed, partial):
    block = pages.pool.shape[1]
    partial[...] = jnp.zeros_like(partial)

    def step(at):
        column = pl.multiple_of(blocks[at] * block, block)
        found = jnp.dot(
            normed[:, pl.ds(column, block)], pages.buffer[at], preferred_element_type=F32
        )
        put(partial, 0, place[...], at, found)

    pages.each(step)


def shrink_kernel(
    count, slots, blocks, core, place, same, other, gain, pool, normed, partial, kept, buffer, sems, raw
):
    pages = Pages(count, slots, pool, buffer, sems, 0)
    pages.start()
    block = pool.shape[1]
    half = same.shape[0]
    for start, state in ((core[0], same), (1 - core[0], other)):
        into = pl.ds(pl.multiple_of(start * half, half), half)
        raw[into, :] = state[...]
        normalise(state, into, gain, normed)
    shrink_pages(pages, blocks, place, normed, partial)

    def keep(chunk, carry):
        for inner in range(CHUNK):
            at = chunk * CHUNK + inner
            column = pl.multiple_of(blocks[at] * block, block)
            put(kept, 0, place[...], at, raw[:, pl.ds(column, block)])
        return carry

    lax.fori_loop(0, pages.chunks, keep, 0)


def norm_and_shrink(count, slots, blocks, core, place, same, other, gain, pool):
    rows, width = place.shape[0], same.shape[1]
    _, block, ranks = pool.shape
    out_shape = (
        jax.ShapeDtypeStruct((rows, width), BF16),
        jax.ShapeDtypeStruct((rows, ranks), F32),
        jax.ShapeDtypeStruct((rows, block), BF16),
    )
    return on_pages(
        shrink_kernel,
        out_shape,
        [count, slots, blocks, core],
        [place, same, other, gain],
        pool,
        (0, ranks),
        "norm_and_shrink",
        [pltpu.VMEM((rows, width), BF16)],
    )


def blocks_kernel(
    count, slots, blocks, came, place, same, other, gain, pool, normed, partial, state, buffer, sems, raw
):
    pages = Pages(count, slots, pool, buffer, sems, 0)
    pages.start()
    chips, rows, block = same.shape

    def sort(chip, carry):
        for which, part in enumerate((same, other)):
            found = part[chip].astype(F32)
            for row in range(rows):
                at = pl.multiple_of(came[which * chips + chip, row] * block, block)
                raw[row : row + 1, pl.ds(at, block)] = found[row : row + 1]
        return carry

    lax.fori_loop(0, chips, sort, 0)
    state[...] = raw[...].astype(BF16)
    normalise(raw, slice(None), gain, normed)
    shrink_pages(pages, blocks, place, normed, partial)


def sort_norm_and_shrink(count, slots, blocks, came, place, same, other, gain, pool):
    chips, rows, block = same.shape
    width = 2 * chips * block
    ranks = pool.shape[2]
    out_shape = (
        jax.ShapeDtypeStruct((rows, width), BF16),
        jax.ShapeDtypeStruct((rows, ranks), F32),
        jax.ShapeDtypeStruct((rows, width), BF16),
    )
    return on_pages(
        blocks_kernel,
        out_shape,
        [count, slots, blocks, came],
        [place, same, other, gain],
        pool,
        (0, ranks),
        "sort_norm_and_shrink",
        [pltpu.VMEM((rows, width), F32)],
    )


def expand_kernel(width, limits, count, slots, blocks, place, shares, pool, terms, buffer, sems):
    pages = Pages(count, slots, pool, buffer, sems, 0)
    pages.start()
    rows = terms.shape[0]
    shrink = jnp.sum(shares[...].astype(F32), axis=0).astype(BF16)
    stacked = jnp.concatenate([shrink[:, :RANK], shrink[:, RANK:]], axis=0)
    lane = lax.broadcasted_iota(jnp.int32, (1, width), 1)
    terms[...] = jnp.zeros_like(terms)

    def step(at):
        found = jnp.dot(stacked, buffer[at, :, :width], preferred_element_type=F32)
        first = blocks[at] * width
        border = jnp.where(first < limits[0], limits[0], limits[1])
        later = (first + lane >= border) | (first >= limits[1])
        chosen = jnp.where(later, found[rows:], found[:rows])
        put(terms, 0, place[...], at, chosen)

    pages.each(step)


def expand(width, limits, count, slots, blocks, place, shares, pool):
    return on_pages(
        functools.partial(expand_kernel, width, limits),
        jax.ShapeDtypeStruct((place.shape[0], width), F32),
        [count, slots, blocks],
        [place, shares],
        pool,
        lane_window(0, width, pool.shape[2]),
        "expand_joint",
    )


def out_shrink_kernel(first, count, slots, place, picked, pool, partial, buffer, sems, total):
    pages = Pages(count, slots, pool, buffer, sems, first)
    pages.start()
    total[...] = jnp.zeros_like(total)

    def step(at):
        found = jnp.dot(picked[...], buffer[at], preferred_element_type=F32)
        put(total, 0, place[...], at, found)

    pages.each(step)
    partial[...] = total[:, total.shape[1] - RANK :]


def out_shrink_partial(count, slots, place, picked, pool):
    window = lane_window(pool.shape[2] - RANK, RANK, pool.shape[2])
    rows = picked.shape[0]
    return on_pages(
        functools.partial(out_shrink_kernel, window[0]),
        jax.ShapeDtypeStruct((rows, RANK), F32),
        [count, slots],
        [place, picked],
        pool,
        window,
        "out_shrink",
        [pltpu.VMEM((rows, window[1]), F32)],
    )


def project_kernel(
    first, count, slots, route, place, heads, picked, weight, pool, routed, partial, *scratch
):
    buffer, sems, tiles, tile_sems, total = scratch
    shards, depth, block = tiles.shape

    def tile(at):
        return pltpu.make_async_copy(
            weight.at[:, pl.ds(pl.multiple_of(at * block, block), block)],
            tiles.at[at],
            tile_sems.at[at],
        )

    def begin(at, carry):
        tile(at).start()
        return carry

    lax.fori_loop(0, shards, begin, 0)
    pages = Pages(count, slots, pool, buffer, sems, first)
    pages.start()

    def multiply(group, carry):
        for inner in range(CHUNK):
            at = group * CHUNK + inner
            tile(at).wait()
            found = jnp.dot(heads[...], tiles[at], preferred_element_type=F32)
            for row in range(found.shape[0]):
                routed[route[at, row], row : row + 1, :] = found[row : row + 1]
        return carry

    lax.fori_loop(0, shards // CHUNK, multiply, 0)
    total[...] = jnp.zeros_like(total)

    def step(at):
        found = jnp.dot(picked[...], buffer[at], preferred_element_type=F32)
        put(total, 0, place[...], at, found)

    pages.each(step)
    partial[...] = total[:, total.shape[1] - RANK :]


def project_and_shrink(count, slots, route, place, heads, picked, weight, pool):
    rows, depth = heads.shape
    shards = route.shape[0]
    block = weight.shape[1] // shards
    used = slots.shape[0]
    window = lane_window(pool.shape[2] - RANK, RANK, pool.shape[2])
    vmem, hbm = pl.BlockSpec(memory_space=pltpu.VMEM), pl.BlockSpec(memory_space=pltpu.HBM)
    return pl.pallas_call(
        functools.partial(project_kernel, window[0]),
        out_shape=(
            jax.ShapeDtypeStruct((shards, rows, block), F32),
            jax.ShapeDtypeStruct((rows, RANK), F32),
        ),
        in_specs=[pl.BlockSpec(memory_space=pltpu.SMEM)] * 3 + [vmem] * 3 + [hbm] * 2,
        out_specs=[vmem] * 2,
        scratch_shapes=[
            pltpu.VMEM((used, pool.shape[1], window[1]), pool.dtype),
            pltpu.SemaphoreType.DMA((used // CHUNK,)),
            pltpu.VMEM((shards, depth, block), weight.dtype),
            pltpu.SemaphoreType.DMA((shards,)),
            pltpu.VMEM((rows, window[1]), F32),
        ],
        compiler_params=pltpu.CompilerParams(vmem_limit_bytes=VMEM_LIMIT),
        cost_estimate=pl.CostEstimate(
            flops=2 * rows * weight.size, bytes_accessed=2 * weight.size, transcendentals=0
        ),
        name="project_and_shrink",
    )(count, slots, route, place, heads, picked, weight, pool)


def finish_kernel(first, count, slots, place, shrink, base, kept, pool, state, buffer, sems, total):
    pages = Pages(count, slots, pool, buffer, sems, first)
    pages.start()
    width = total.shape[1]
    inside = buffer.shape[2] - width
    total[...] = base[...] + kept[...].astype(F32)

    def step(at):
        found = jnp.dot(shrink[...], buffer[at, :, inside:], preferred_element_type=F32)
        put(total, 0, place[...], at, found, add=True)

    pages.each(step)
    state[...] = total[...].astype(BF16)


def finish_blocks(count, slots, place, shrink, base, kept, pool):
    rows, width = base.shape
    window = lane_window(pool.shape[2] - width, width, pool.shape[2])
    return on_pages(
        functools.partial(finish_kernel, window[0]),
        jax.ShapeDtypeStruct((rows, width), BF16),
        [count, slots],
        [place, shrink, base, kept],
        pool,
        window,
        "finish_blocks",
        [pltpu.VMEM((rows, width), F32)],
    )


def out_expand_kernel(
    first, width, count, slots, blocks, core, place, shares, base, pool, keep, sent, buffer, sems, shrink, send
):
    pages = Pages(count, slots, pool, buffer, sems, first)
    pages.start()
    half = keep.shape[0]
    inside = buffer.shape[2] - width
    shrink[...] = jnp.sum(shares[...].astype(F32), axis=0)
    mine = pl.multiple_of(core[0] * half, half)
    other = pl.multiple_of((1 - core[0]) * half, half)
    ordered = [shrink[pl.ds(start, half), :].astype(BF16) for start in (mine, other)]
    ordered = jnp.concatenate(ordered, axis=0)
    keep[...] = base[pl.ds(mine, half), :]
    send[...] = base[pl.ds(other, half), :]

    def step(at):
        found = jnp.dot(ordered, buffer[at, :, inside:], preferred_element_type=F32)
        column = blocks[at] * width
        put(keep, column, place[pl.ds(mine, half), :], at, found[:half], add=True)
        put(send, column, place[pl.ds(other, half), :], at, found[half:], add=True)

    pages.each(step)
    sent[...] = send[...].astype(BF16)


def out_expand(width, count, slots, blocks, core, place, shares, base, pool):
    rows = place.shape[0]
    half = (rows // 2, base.shape[1])
    window = lane_window(pool.shape[2] - width, width, pool.shape[2])
    return on_pages(
        functools.partial(out_expand_kernel, window[0], width),
        (jax.ShapeDtypeStruct(half, F32), jax.ShapeDtypeStruct(half, BF16)),
        [count, slots, blocks, core],
        [place, shares, base],
        pool,
        window,
        "expand_out",
        [pltpu.VMEM((rows, RANK), F32), pltpu.VMEM(half, F32)],
    )


def attend_kernel(
    from_parts, holders, wanted, lengths, joint, turn, cached, *refs
):
    older, (parts, fresh, heads, mixed) = refs[:-4], refs[-4:]
    row_count, positions = cached.shape[0], cached.shape[1]
    group = HEADS // KVH
    shards, block = parts.shape[0], parts.shape[2] // 2
    if from_parts:
        piece = joint.shape[2] // 2
        per = piece // HD
        for at in range(shards):
            base = joint[at, :, :piece].astype(F32)
            for row in range(row_count):
                terms = joint[holders[row, at], :, piece:].astype(F32)
                summed = base[row : row + 1] + terms[row : row + 1]
                for inner in range(per):
                    heads[row, at * per + inner : at * per + inner + 1, :] = summed[
                        :, inner * HD : (inner + 1) * HD
                    ]
    else:
        heads[...] = joint[...]
    scaling = HD ** (-0.5)
    column = lax.broadcasted_iota(jnp.int32, (HEADS, positions), 1)
    for row in range(row_count):
        rounded = heads[row].astype(BF16).astype(F32)
        plain = rounded[: HEADS + KVH]
        turned = plain * turn[row, 0:1, :] + pltpu.roll(plain, HD // 2, 1) * turn[row, 1:2, :]
        turned = turned.astype(BF16)
        fresh[row, 0] = turned[HEADS:].astype(F32)
        fresh[row, 1] = rounded[HEADS + KVH :]
        queries = turned[:HEADS]
        scores = jnp.concatenate(
            [
                lax.dot_general(
                    queries[g * group : (g + 1) * group],
                    cached[row, :, g * HD : (g + 1) * HD],
                    (((1,), (1,)), ((), ())),
                    preferred_element_type=F32,
                )
                for g in range(KVH)
            ],
            axis=0,
        )
        scores = jnp.where(column < lengths[row], scores * scaling, -jnp.inf)
        steps = [old[row] for old in older] + [fresh[row]]

        def spread(values):
            return jnp.concatenate(
                [jnp.broadcast_to(values[g : g + 1], (group, HD)) for g in range(KVH)], axis=0
            )

        wide = queries.astype(F32)
        extra = [
            jnp.sum(wide * spread(step[0]), axis=1, keepdims=True) * scaling for step in steps
        ]
        highest = jnp.max(scores, axis=1, keepdims=True)
        for one in extra:
            highest = jnp.maximum(highest, one)
        exps = jnp.exp(scores - highest)
        extra = [jnp.exp(one - highest) for one in extra]
        total = jnp.sum(exps, axis=1, keepdims=True)
        for one in extra:
            total = total + one
        weights = (exps / total).astype(BF16)
        result = jnp.concatenate(
            [
                jnp.dot(
                    weights[g * group : (g + 1) * group],
                    cached[row, :, (KVH + g) * HD : (KVH + g + 1) * HD],
                    preferred_element_type=F32,
                )
                for g in range(KVH)
            ],
            axis=0,
        )
        for one, step in zip(extra, steps):
            result = result + (one / total).astype(BF16).astype(F32) * spread(step[1])
        for at in range(shards):
            for inner in range(block // HD):
                head = at * (block // HD) + inner
                mixed[row, at, 0:1, inner * HD : (inner + 1) * HD] = result[head : head + 1]
    for at in range(shards):
        plain = [mixed[row, at, 0:1, :] for row in range(row_count)]
        picked = [mixed[row, wanted[row, at], 0:1, :] for row in range(row_count)]
        parts[at] = jnp.concatenate(
            [jnp.concatenate(plain, axis=0), jnp.concatenate(picked, axis=0)], axis=1
        ).astype(BF16)


def attend(from_parts, shards, block, holders, wanted, lengths, joint, turn, cached, older):
    row_count = cached.shape[0]
    vmem = pl.BlockSpec(memory_space=pltpu.VMEM)
    return pl.pallas_call(
        functools.partial(attend_kernel, from_parts),
        out_shape=(
            jax.ShapeDtypeStruct((shards, row_count, 2 * block), BF16),
            jax.ShapeDtypeStruct((row_count, 2, KVH, HD), F32),
        ),
        in_specs=[pl.BlockSpec(memory_space=pltpu.SMEM)] * 3 + [vmem] * (3 + len(older)),
        out_specs=[vmem] * 2,
        scratch_shapes=[
            pltpu.VMEM((row_count, HEADS + 2 * KVH, HD), F32),
            pltpu.VMEM((row_count, shards, 8, block), F32),
        ],
        compiler_params=pltpu.CompilerParams(vmem_limit_bytes=VMEM_LIMIT),
        cost_estimate=pl.CostEstimate(
            flops=0, bytes_accessed=2 * cached.size, transcendentals=0
        ),
        name="attend",
    )(holders, wanted, lengths, joint, turn, cached, *older)


def exchange(parts, groups=None):
    return lax.all_to_all(
        parts, "tp", split_axis=0, concat_axis=0, tiled=True, axis_index_groups=groups
    )


def body(
    hidden,
    norm_gain,
    qkv_weight,
    out_weight,
    key_values,
    cache_lengths,
    adapter_ids,
    page_table,
    down_pages,
    up_pages,
):
    shards = lax.axis_size("tp")
    me = lax.axis_index("tp")
    rows_dev, width = hidden.shape
    rows = rows_dev * shards
    qkv_slice = qkv_weight.shape[1]
    slice_width = out_weight.shape[0]
    adapters = page_table.shape[0]
    key_limit = width + KVH * HD
    chips = shards // 2
    core = me % 2
    chip = me // 2
    same_core = [[2 * at + which for at in range(chips)] for which in range(2)]

    def by_core(values, axis=0):
        shape = values.shape
        values = values.reshape(shape[:axis] + (chips, 2, rows_dev) + shape[axis + 1 :])
        return jnp.swapaxes(values, axis, axis + 1).reshape(shape)

    def by_device(values):
        values = values.reshape((2, chips, rows_dev) + values.shape[1:])
        return jnp.swapaxes(values, 0, 1).reshape((shards, rows_dev) + values.shape[3:])

    def swap_bits(values, bits):
        return lax.ppermute(values, "tp", [(at, at ^ bits) for at in range(shards)])

    def same_rows(own):
        return exchange(jnp.broadcast_to(own[None], (chips,) + own.shape), same_core)

    def scatter_rows(keep, send):
        summed = keep + swap_bits(send, 1).astype(F32)
        four = summed.reshape(chips // 4, 4, rows_dev, width)
        here = chip & 3
        total = lax.dynamic_index_in_dim(four, here, 1, keepdims=False)
        arrived = [
            swap_bits(
                lax.dynamic_index_in_dim(four, here ^ step, 1, keepdims=False).astype(BF16),
                2 * step,
            )
            for step in range(1, 4)
        ]
        for part in arrived:
            total = total + part.astype(F32)
        for bit in reversed(range(2, chips.bit_length() - 1)):
            here = (chip >> bit) & 1
            pair = total.reshape(2, -1, rows_dev, width)
            total = lax.dynamic_index_in_dim(pair, here, 0, keepdims=False)
            away = lax.dynamic_index_in_dim(pair, 1 - here, 0, keepdims=False)
            total = total + swap_bits(away.astype(BF16), 2 << bit).astype(F32)
        return total.reshape(rows_dev, width)

    def scatter_blocks(routed, extra):
        tail = extra.shape[0]

        def trade(away, bits):
            message = jnp.concatenate([away.reshape(-1, slice_width), extra], axis=0)
            arrived = swap_bits(message.astype(BF16), bits).astype(F32)
            return arrived[:-tail].reshape(away.shape), arrived[-tail:]

        arrived, more = trade(routed[chips:], 1)
        four = (routed[:chips] + arrived).reshape(chips // 4, 4, rows, slice_width)
        extra = extra + more
        here = chip & 3
        total = lax.dynamic_index_in_dim(four, here, 1, keepdims=False)
        traded = [
            trade(lax.dynamic_index_in_dim(four, here ^ step, 1, keepdims=False), 2 * step)
            for step in range(1, 4)
        ]
        for arrived, more in traded:
            total, extra = total + arrived, extra + more
        for bit in reversed(range(2, chips.bit_length() - 1)):
            here = (chip >> bit) & 1
            pair = total.reshape(2, -1, rows, slice_width)
            away = lax.dynamic_index_in_dim(pair, 1 - here, 0, keepdims=False)
            arrived, more = trade(away, 2 << bit)
            total = lax.dynamic_index_in_dim(pair, here, 0, keepdims=False) + arrived
            extra = extra + more
        return total.reshape(rows, slice_width), extra

    def to_all(partial):
        return exchange(jnp.broadcast_to(partial.astype(BF16)[None], (shards,) + partial.shape))

    device_iota = jnp.arange(shards, dtype=jnp.int32)
    adapter_iota = jnp.arange(adapters, dtype=jnp.int32)
    core_of = core.astype(jnp.int32).reshape(1)
    gain = norm_gain.reshape(1, width)

    def choose(ids):
        return (ids[:, :, None] == adapter_iota).astype(jnp.int32)

    def blocks_at(owners):
        return jnp.sum((owners[:, :, None] == device_iota) * device_iota[None, :, None], axis=1)

    owner_dev = page_table // adapters
    held_here = (owner_dev == me).astype(jnp.int32)
    block_here = jnp.sum(held_here * device_iota, axis=1)
    slot_here = jnp.sum(held_here * (page_table % adapters), axis=1)
    chosen = choose(adapter_ids)
    in_use = jnp.max(chosen, axis=1)
    rank = jnp.sum(in_use[:, None, :] * (adapter_iota[None, :] <= adapter_iota[:, None]), axis=-1) - 1
    listed = min(adapters, rows)
    named = in_use[:, None, :] * (rank[:, None, :] == jnp.arange(listed, dtype=jnp.int32)[:, None])
    count = jnp.sum(in_use, axis=1, keepdims=True)
    use_block = jnp.sum(named * block_here, axis=-1)
    slots = jnp.sum(named * slot_here, axis=-1)
    place = by_core(jnp.sum(chosen * rank[:, None, :], axis=-1), 1)
    place = jnp.broadcast_to(place[:, :, None], (STEPS, rows, LANES))
    block_of = by_core(jnp.sum(chosen[:, None] * blocks_at(owner_dev).T[:, None], axis=-1), 2)
    only_query = block_of * qkv_slice < width
    came = jnp.swapaxes(block_of[0].reshape(chips, 2, rows), 0, 1)
    came = jnp.where(core == 0, came, came[::-1]).reshape(shards, rows)
    holds = by_core(jnp.sum(chosen[0][:, :, None] * owner_dev, axis=1)).T
    route = ((holds % 2) ^ core) * chips + holds // 2

    mine = lax.dynamic_slice_in_dim(chosen, me * rows_dev, rows_dev, 1)
    holders = jnp.sum(mine[:, :, :, None] * owner_dev, axis=2)
    wanted = jnp.sum(mine[:, :, :, None] * blocks_at(owner_dev), axis=2)
    position = cache_lengths[None, :] + jnp.arange(STEPS, dtype=jnp.int32)[:, None]
    frequency = rope_base ** (-(jnp.arange(HD // 2, dtype=F32) * 2.0) / HD)
    angles = position.astype(F32)[:, :, None] * frequency
    cosine, sine = jnp.cos(angles), jnp.sin(angles)
    turn = jnp.stack(
        [
            jnp.concatenate([cosine, cosine], axis=-1),
            jnp.concatenate([-sine, sine], axis=-1),
        ],
        axis=2,
    )
    tables = [(holders[step], wanted[step], turn[step]) for step in range(STEPS)]
    tables.append((came, route))

    residual = hidden
    older = []
    from_parts = qkv_slice % LANES == 0
    for decode_step in range(STEPS):
        use = [count[decode_step], slots[decode_step]]
        blocks = use_block[decode_step]
        spot = place[decode_step]
        same = same_rows(residual)
        if decode_step == 0:
            same, tables = lax.optimization_barrier((same, tables))
            came, route = tables[-1]
        other = swap_bits(same, 1)
        if decode_step == 0:
            halves = [part.reshape(rows // 2, width) for part in (same, other)]
            normed, partial, kept = norm_and_shrink(
                *use, blocks, core_of, spot, *halves, gain, down_pages
            )
        else:
            normed, partial, state = sort_norm_and_shrink(
                *use, blocks, came, spot, same, other, gain, down_pages
            )
        kinds = partial[:, : 3 * RANK].astype(BF16)
        early = kinds[None, :, : 2 * RANK]
        late = kinds[None, :, RANK:]
        shares = exchange(jnp.where(only_query[decode_step][:, :, None], early, late))
        projected = jnp.dot(normed, qkv_weight, preferred_element_type=F32)
        terms = expand(qkv_slice, (width, key_limit), *use, blocks, spot, shares, up_pages)
        message = by_device(jnp.concatenate([projected, terms], axis=1).astype(BF16))
        arrived = exchange(message)
        holders, wanted, turn = tables[decode_step]
        if not from_parts:
            by_row = jnp.swapaxes(arrived, 0, 1).astype(F32)
            arrived = by_row[:, :, :qkv_slice] + jnp.take_along_axis(
                by_row[:, :, qkv_slice:], holders[:, :, None], axis=1
            )
            arrived = arrived.reshape(rows_dev, HEADS + 2 * KVH, HD)
        parts, fresh = attend(
            from_parts,
            shards,
            slice_width,
            holders,
            wanted,
            cache_lengths,
            arrived,
            turn,
            key_values,
            older,
        )
        older.append(fresh)
        headwise = by_core(exchange(parts).reshape(rows, 2 * slice_width))
        heads, picked = headwise[:, :slice_width], headwise[:, slice_width:]
        if decode_step < STEPS - 1:
            routed, partial = project_and_shrink(
                *use, route, spot, heads, picked, out_weight, down_pages
            )
            fold = slice_width // RANK
            partial = partial.reshape(fold, rows // fold, RANK)
            partial = jnp.swapaxes(partial, 0, 1).reshape(rows // fold, slice_width)
            base, shrink = scatter_blocks(routed, partial)
            shrink = jnp.swapaxes(shrink.reshape(rows // fold, fold, RANK), 0, 1)
            shrink = shrink.reshape(rows, RANK).astype(BF16)
            residual = finish_blocks(*use, spot, shrink, base, kept, up_pages)
        else:
            out_shares = to_all(out_shrink_partial(*use, spot, picked, down_pages))
            base = jnp.dot(heads, out_weight, preferred_element_type=F32)
            keep, send = out_expand(
                slice_width, *use, blocks, core_of, spot, out_shares, base, up_pages
            )
            own = core * (rows // 2) + chip * rows_dev
            own = lax.dynamic_slice_in_dim(state, own, rows_dev, 0)
            residual = (own.astype(F32) + scatter_rows(keep, send)).astype(BF16)
    return residual


def solution(mesh):
    in_specs = (
        P(("cells", "tp"), None),
        P(),
        P(None, "tp"),
        P("tp", None),
        P(("cells", "tp"), None, None),
        P(("cells", "tp")),
        P(None, "cells"),
        P("cells", None),
        P("tp", None, None),
        P("tp", None, None),
    )
    out_specs = P(("cells", "tp"), None)
    return jax.shard_map(body, mesh=mesh, in_specs=in_specs, out_specs=out_specs, check_vma=False)
```

time: 1730 us -> 177 us (0.10)
  blocking collectives: 1010 us -> 51.1 us
  waiting for transfers between devices: 294 us -> 26.4 us
  local copies, waits for them, and re-layouts: 206 us -> 6.62 us
  starting transfers between devices: 104 us -> 28.9 us
  other arithmetic: 52.7 us -> 9.43 us
  Pallas kernels: 0 us -> 36.3 us
  matrix products: 45 us -> 16.3 us
    all_gather x2 -> x0, blocking collectives: 662 us -> none  [body(): project_portion = lax.all_gather(normed, 'tp', axis=0, tiled=True)]
    psum x4 -> x0, blocking collectives: 337 us -> none  [the longest x2 212 us: body(): shrink = lax.psum(joined[:, qkv_slice:], 'tp').astype(jnp.bfloat16)]
    all_to_all x7 -> x4, waiting for transfers between devices: 265 us -> 7.91 us  [exchange(): lax.all_to_all(parts, 'tp', split_axis=0, concat_axis=0, tiled=True, axis...]
    gather x12 -> x0, local copies, waits for them, and re-layouts: 95.4 us -> none  [the longest x2 23.6 us: outgoing(): ordered = jnp.take(pages, held_slot, axis=0)]
    all_to_all x7 -> x4, starting transfers between devices: 104 us -> 19.1 us  [exchange(): lax.all_to_all(parts, 'tp', split_axis=0, concat_axis=0, tiled=True, axis...]
    scatter x2 -> x0, local copies, waits for them, and re-layouts: 65.7 us -> none  [outgoing(): return zeroed.at[send_row].set(ordered)]
    select_n x7 -> x3, other arithmetic: 45.6 us -> 1.58 us  [the longest x2 1.58 us: body(): jnp.where(only_query[decode_step][:, :, None], early, late)]
    all_to_all x1 -> x5, blocking collectives: 9.48 us -> 51.1 us  [exchange(): lax.all_to_all(parts, 'tp', split_axis=0, concat_axis=0, tiled=True, axis...]
  transfers between devices with their start and end apart: 9 -> 16, of which waited for: 5 -> 14; matrix products, arithmetic and copies ran while one was open for 10% -> 14% of each run, Pallas kernels for 0% -> 0%
where the time goes in v1:
time: 177 us; the launch traced here: 176 us
  blocking collectives  51.1 us (29%)
  Pallas kernels  36.3 us (21%)
  starting transfers between devices  28.9 us (16%)
  waiting for transfers between devices  26.4 us (15%)
  matrix products  16.3 us (9%)
  other arithmetic  9.43 us (5%)
  local copies, waits for them, and re-layouts  6.62 us (4%)
    all_to_all x5, blocking collectives, exchange(): lax.all_to_all(parts, 'tp', split_axis=0, concat_axis=0, tiled=True, axis...  51.1 us
    pallas_call x7, Pallas kernels, on_pages(): pl.pallas_call(kernel, out_shape=out_shape, in_specs=[pl.BlockSpec(memory...  26.1 us
    all_to_all x4, starting transfers between devices, exchange(): lax.all_to_all(parts, 'tp', split_axis=0, concat_axis=0, tiled=True, axis...  19.1 us
    ppermute x12, waiting for transfers between devices, swap_bits(): return lax.ppermute(values, 'tp', [(at, at ^ bits) for at in range(shards)])  18.4 us
    dot_general x2, matrix products, body(): projected = jnp.dot(normed, qkv_weight, preferred_element_type=F32)  11.4 us
    ppermute x12, starting transfers between devices, swap_bits(): return lax.ppermute(values, 'tp', [(at, at ^ bits) for at in range(shards)])  9.84 us
    all_to_all x4, waiting for transfers between devices, exchange(): lax.all_to_all(parts, 'tp', split_axis=0, concat_axis=0, tiled=True, axis...  7.91 us
    pallas_call x1, Pallas kernels, project_and_shrink(): pl.pallas_call(functools.partial(project_kernel, window[0]), out_shape=(j...  7.15 us
  transfers between devices with their start and end apart: 16, of which 14 were waited for; matrix products, arithmetic and copies ran while one was open for 14% of the time, Pallas kernels for 0%

profile of v1, /device:TPU:0, one launch (start us, length us, event | category | flops | bytes accessed | tf_op | source)
XLA Modules:
  0.0 175.9 jit_solution(14422367184626759844)
XLA Ops:
  0.0 1.6 broadcast_in_dim.57
  1.6 7.3 %all-to-all-start = ((bf16[8,2,8192]{2,1,0:T(2,128)(2,1)}), bf16[8,2,8192]{2,1,0:T(2,128)(2,1)S(1)}, u32[]{:S(2)}, u32[]{:S(2)}) async-start(bf16[8,2,8192]{2,1,0:T(2,128)(2,1)} %broadcast_in_dim.57), calls=%async_computation | async-start | bytes 524288 | tf_op jit(solution)/shard_map/all_to_all | solution.py:530
  8.9 0.8 fusion.15
  9.7 0.8 fusion.13
  15.0 0.9 fusion.9
  16.1 1.7 all-to-all-done
  18.5 0.7 reshape.220.gain
  19.7 4.2 %norm_and_shrink.1 = (bf16[32,8192]{1,0:T(8,128)(2,1)S(1)}, f32[32,256]{1,0:T(8,128)S(1)}, bf16[32,512]{1,0:T(8,128)(2,1)S(1)}) custom-call(s32[1]{0:T(128)} %get-tuple-element.92.count, s32[32]{0:T(128)S(1)} %get-tuple-element.95.slots, s32[32]{0:T(128)S(1)} %get-tuple-element.88.blocks, s32[1]{0:T(128)} %bitcast.24.core, ...), custom_call_target="tpu_custom_call" | custom-call | bytes 8388608 | tf_op jit(solution)/shard_map/norm_and_shrink/pallas_call | solution.py:70
  24.0 0.8 broadcast_select_fusion.1
  24.8 4.6 %all-to-all-start.1 = ((bf16[16,32,128]{2,1,0:T(8,128)(2,1)}), bf16[16,32,128]{2,1,0:T(8,128)(2,1)S(1)}, u32[]{:S(2)}, u32[]{:S(2)}) async-start(bf16[16,32,128]{2,1,0:T(8,128)(2,1)} %broadcast_select_fusion.1), calls=%async_computation.1 | async-start | bytes 262144 | tf_op jit(solution)/shard_map/all_to_all | solution.py:530
  29.4 5.7 %convolution_convert_fusion.1 = bf16[32,640]{1,0:T(8,128)(2,1)S(1)} fusion(bf16[32,8192]{1,0:T(8,128)(2,1)S(1)} %get-tuple-element.32, bf16[8192,640]{1,0:T(8,128)(2,1)} %param.12), kind=kOutput, calls=%fused_computation.1 | convolution fusion | flops 335564800 | bytes 11051008 | tf_op jit(solution)/shard_map/dot_general | solution.py:702
  35.2 2.1 %all-to-all-done.1.shares = bf16[16,32,128]{2,1,0:T(8,128)(2,1)S(1)} async-done(((bf16[16,32,128]{2,1,0:T(8,128)(2,1)}), bf16[16,32,128]{2,1,0:T(8,128)(2,1)S(1)}, u32[]{:S(2)}, u32[]{:S(2)}) %all-to-all-start.1) | async-done | bytes 131104 | tf_op jit(solution)/shard_map/all_to_all | solution.py:530
  37.3 3.4 %expand_joint.2 = f32[32,640]{1,0:T(8,128)S(1)} custom-call(s32[1]{0:T(128)} %get-tuple-element.92.count, s32[32]{0:T(128)S(1)} %get-tuple-element.95.slots, s32[32]{0:T(128)S(1)} %get-tuple-element.88.blocks, s32[32,128]{1,0:T(8,128)S(1)} %broadcast_in_dim.61.place, bf16[16,32,128]{2,1,0:T(8,128)(2,1)S(1)} %all-to-all-done.1.shares, bf16[64,64,1152]{2,1,0:T(8,128)(2,1)} %pool.15), custom_call_target="tpu_custom_call" | custom-call | bytes 2621440 | tf_op jit(solution)/shard_map/expand_joint/pallas_call | solution.py:70
  41.0 10.8 %all_to_all.45.joint = bf16[16,2,1280]{2,1,0:T(2,128)(2,1)S(1)} all-to-all(bf16[16,2,1280]{2,1,0:T(2,128)(2,1)S(1)} %bitcast.161), channel_id=1, replica_groups=mesh['cells'=2,'tp'=16] {'tp'}, dimensions={0} | all-to-all | bytes 163840 | tf_op jit(solution)/shard_map/all_to_all | solution.py:530
  51.8 1.5 attend.2
  53.3 9.5 %all_to_all.46 = bf16[16,2,1024]{2,1,0:T(2,128)(2,1)S(1)} all-to-all(bf16[16,2,1024]{2,1,0:T(2,128)(2,1)S(1)} %get-tuple-element.35), channel_id=1, replica_groups=mesh['cells'=2,'tp'=16] {'tp'}, dimensions={0} | all-to-all | bytes 131072 | tf_op jit(solution)/shard_map/all_to_all | solution.py:530
  62.9 7.1 %project_and_shrink.1 = (f32[16,32,512]{2,1,0:T(8,128)S(1)}, f32[32,64]{1,0:T(8,128)S(1)}) custom-call(s32[1]{0:T(128)} %get-tuple-element.92.count, s32[32]{0:T(128)S(1)} %get-tuple-element.95.slots, s32[16,32]{1,0:T(8,128)S(1)} %fusion.20.route, s32[32,128]{1,0:T(8,128)S(1)} %broadcast_in_dim.61.place, bf16[32,512]{1,0:T(8,128)(2,1)S(1)} %get-tuple-element.67.heads, ...), custom_call_target="tpu_custom_call" | custom-call | flops 268435456 | bytes 8388608 | tf_op jit(solution)/shard_map/project_and_shrink/pallas_call | solution.py:323
  70.3 1.5 collective-permute-done.1
  72.4 1.4 collective-permute-start.3
  73.8 1.9 %collective-permute-start.2 = (bf16[68,512]{1,0:T(8,128)(2,1)S(1)}, bf16[68,512]{1,0:T(8,128)(2,1)S(1)}, u32[]{:S(2)}, u32[]{:S(2)}) collective-permute-start(bf16[68,512]{1,0:T(8,128)(2,1)S(1)} %get-tuple-element.76), channel_id=1, source_target_pairs={{0,2},{1,3},{2,0},{3,1},{4,6},{5,7},{6,4},{7,5},{8,10},{9,11},{10,... | collective-permute-start | bytes 208904 | tf_op jit(solution)/shard_map/ppermute | solution.py:570
  75.7 2.5 %collective-permute-done.4 = bf16[68,512]{1,0:T(8,128)(2,1)S(1)} collective-permute-done((bf16[68,512]{1,0:T(8,128)(2,1)S(1)}, bf16[68,512]{1,0:T(8,128)(2,1)S(1)}, u32[]{:S(2)}, u32[]{:S(2)}) %collective-permute-start.4) | collective-permute-done | bytes 69664 | tf_op jit(solution)/shard_map/ppermute | solution.py:570
  78.2 0.7 collective-permute-done.2
  79.4 4.7 %collective-permute-done.5 = bf16[36,512]{1,0:T(8,128)(2,1)S(1)} collective-permute-done((bf16[36,512]{1,0:T(8,128)(2,1)S(1)}, bf16[36,512]{1,0:T(8,128)(2,1)S(1)}, u32[]{:S(2)}, u32[]{:S(2)}) %collective-permute-start.5) | collective-permute-done | bytes 36896 | tf_op jit(solution)/shard_map/ppermute | solution.py:570
  84.3 3.1 %finish_blocks.1 = bf16[32,512]{1,0:T(8,128)(2,1)S(1)} custom-call(s32[1]{0:T(128)} %get-tuple-element.92.count, s32[32]{0:T(128)S(1)} %get-tuple-element.95.slots, s32[32,128]{1,0:T(8,128)S(1)} %broadcast_in_dim.61.place, bf16[32,64]{1,0:T(8,128)(2,1)S(1)} %bitcast.152, f32[32,512]{1,0:T(8,128)S(1)} %slice_add_fusion.1.base, ...), custom_call_target="tpu_custom_call" | custom-call | bytes 2097152 | tf_op jit(solution)/shard_map/finish_blocks/pallas_call | solution.py:70
  87.4 10.6 %all_to_all.47.same = bf16[8,32,512]{2,1,0:T(8,128)(2,1)S(1)} all-to-all(bf16[8,32,512]{2,1,0:T(8,128)(2,1)S(1)} %broadcast_in_dim.114), channel_id=1, replica_groups={{0,2,4,6,8,10,12,14},{1,3,5,7,9,11,13,15},{16,18,20,22,24,26,28,30},{17..., dimensions={0} | all-to-all | bytes 524288 | tf_op jit(solution)/shard_map/all_to_all | solution.py:530
  98.2 1.3 collective-permute-done.6.other
  99.6 4.5 %sort_norm_and_shrink.1 = (bf16[32,8192]{1,0:T(8,128)(2,1)S(1)}, f32[32,256]{1,0:T(8,128)S(1)}, bf16[32,8192]{1,0:T(8,128)(2,1)S(1)}) custom-call(s32[1]{0:T(128)} %get-tuple-element.93.count, s32[32]{0:T(128)S(1)} %get-tuple-element.94.slots, s32[32]{0:T(128)S(1)} %get-tuple-element.89.blocks, s32[16,32]{1,0:T(8,128)S(1)} %bitcast.151, ...), custom_call_target="tpu_custom_call" | custom-call | bytes 8388608 | tf_op jit(solution)/shard_map/sort_norm_and_shrink/pallas_call | solution.py:70
  104.2 0.8 broadcast_select_fusion
  105.0 3.5 %all-to-all-start.5 = ((bf16[16,32,128]{2,1,0:T(8,128)(2,1)}), bf16[16,32,128]{2,1,0:T(8,128)(2,1)S(1)}, u32[]{:S(2)}, u32[]{:S(2)}) async-start(bf16[16,32,128]{2,1,0:T(8,128)(2,1)} %broadcast_select_fusion), calls=%async_computation.5 | async-start | bytes 262144 | tf_op jit(solution)/shard_map/all_to_all | solution.py:530
  108.5 5.7 %convolution_convert_fusion = bf16[32,640]{1,0:T(8,128)(2,1)S(1)} fusion(bf16[32,8192]{1,0:T(8,128)(2,1)S(1)} %get-tuple-element.42, bf16[8192,640]{1,0:T(8,128)(2,1)} %param.12), kind=kOutput, calls=%fused_computation | convolution fusion | flops 335564800 | bytes 11051008 | tf_op jit(solution)/shard_map/dot_general | solution.py:702
  114.2 2.2 %all-to-all-done.5.shares = bf16[16,32,128]{2,1,0:T(8,128)(2,1)S(1)} async-done(((bf16[16,32,128]{2,1,0:T(8,128)(2,1)}), bf16[16,32,128]{2,1,0:T(8,128)(2,1)S(1)}, u32[]{:S(2)}, u32[]{:S(2)}) %all-to-all-start.5) | async-done | bytes 131104 | tf_op jit(solution)/shard_map/all_to_all | solution.py:530
  116.4 3.6 %expand_joint.3 = f32[32,640]{1,0:T(8,128)S(1)} custom-call(s32[1]{0:T(128)} %get-tuple-element.93.count, s32[32]{0:T(128)S(1)} %get-tuple-element.94.slots, s32[32]{0:T(128)S(1)} %get-tuple-element.89.blocks, s32[32,128]{1,0:T(8,128)S(1)} %broadcast_in_dim.59.place, bf16[16,32,128]{2,1,0:T(8,128)(2,1)S(1)} %all-to-all-done.5.shares, bf16[64,64,1152]{2,1,0:T(8,128)(2,1)} %pool.15), custom_call_target="tpu_custom_call" | custom-call | bytes 2621440 | tf_op jit(solution)/shard_map/expand_joint/pallas_call | solution.py:70
  120.2 10.7 %all_to_all.48.joint = bf16[16,2,1280]{2,1,0:T(2,128)(2,1)S(1)} all-to-all(bf16[16,2,1280]{2,1,0:T(2,128)(2,1)S(1)} %bitcast.162), channel_id=1, replica_groups=mesh['cells'=2,'tp'=16] {'tp'}, dimensions={0} | all-to-all | bytes 163840 | tf_op jit(solution)/shard_map/all_to_all | solution.py:530
  131.0 1.6 attend.3
  132.6 9.5 %all_to_all.49 = bf16[16,2,1024]{2,1,0:T(2,128)(2,1)S(1)} all-to-all(bf16[16,2,1024]{2,1,0:T(2,128)(2,1)S(1)} %get-tuple-element.46), channel_id=1, replica_groups=mesh['cells'=2,'tp'=16] {'tp'}, dimensions={0} | all-to-all | bytes 131072 | tf_op jit(solution)/shard_map/all_to_all | solution.py:530
  142.1 3.7 %out_shrink.1 = f32[32,64]{1,0:T(8,128)S(1)} custom-call(s32[1]{0:T(128)} %get-tuple-element.93.count, s32[32]{0:T(128)S(1)} %get-tuple-element.94.slots, s32[32,128]{1,0:T(8,128)S(1)} %broadcast_in_dim.59.place, bf16[32,512]{1,0:T(8,128)(2,1)S(1)} %slice.199.picked, bf16[64,512,256]{2,1,0:T(8,128)(2,1)} %pool.14), custom_call_target="tpu_custom_call" | custom-call | bytes 4194304 | tf_op jit(solution)/shard_map/out_shrink/pallas_call | solution.py:70
  145.9 0.8 reshape.239
  146.7 3.7 %all-to-all-start.8 = ((bf16[16,2,1024]{2,1,0:T(2,128)(2,1)}), bf16[16,2,1024]{2,1,0:T(2,128)(2,1)S(1)}, u32[]{:S(2)}, u32[]{:S(2)}) async-start(bf16[16,2,1024]{2,1,0:T(2,128)(2,1)} %reshape.239), calls=%async_computation.8 | async-start | bytes 131072 | tf_op jit(solution)/shard_map/all_to_all | solution.py:530
  150.3 4.9 %fusion.11.base = f32[32,8192]{1,0:T(8,128)S(1)} fusion(bf16[512,8192]{1,0:T(8,128)(2,1)} %weight.1, bf16[32,1024]{1,0:T(8,128)(2,1)S(1)} %reshape.236), kind=kOutput, calls=%fused_computation.46 | convolution fusion | flops 268435456 | bytes 9469952 | tf_op jit(solution)/shard_map/dot_general | solution.py:741
  155.3 1.9 %all-to-all-done.8 = bf16[16,2,1024]{2,1,0:T(2,128)(2,1)S(1)} async-done(((bf16[16,2,1024]{2,1,0:T(2,128)(2,1)}), bf16[16,2,1024]{2,1,0:T(2,128)(2,1)S(1)}, u32[]{:S(2)}, u32[]{:S(2)}) %all-to-all-start.8) | async-done | bytes 65568 | tf_op jit(solution)/shard_map/all_to_all | solution.py:530
  157.3 3.6 %expand_out.1 = (f32[16,8192]{1,0:T(8,128)S(1)}, bf16[16,8192]{1,0:T(8,128)(2,1)S(1)}) custom-call(s32[1]{0:T(128)} %get-tuple-element.93.count, s32[32]{0:T(128)S(1)} %get-tuple-element.94.slots, s32[32]{0:T(128)S(1)} %get-tuple-element.89.blocks, s32[1]{0:T(128)} %bitcast.24.core, s32[32,128]{1,0:T(8,128)S(1)} %broadcast_in_dim.59.place, ...), custom_call_target="tpu_custom_call" | custom-call | bytes 2097152 | tf_op jit(solution)/shard_map/expand_out/pallas_call | solution.py:70
  161.0 1.5 collective-permute-done.7
  163.2 1.3 collective-permute-start.9
  164.5 2.1 %collective-permute-start.10 = (bf16[2,2,8192]{2,1,0:T(2,128)(2,1)S(1)}, bf16[2,2,8192]{2,1,0:T(2,128)(2,1)S(1)}, u32[]{:S(2)}, u32[]{:S(2)}) collective-permute-start(bf16[2,2,8192]{2,1,0:T(2,128)(2,1)S(1)} %get-tuple-element.62), channel_id=1, source_target_pairs={{0,6},{1,7},{2,4},{3,5},{4,2},{5,3},{6,0},{7,1},{8,14},{9,15},{10,... | collective-permute-start | bytes 196616 | tf_op jit(solution)/shard_map/ppermute | solution.py:570
  166.6 0.8 collective-permute-done.8
  168.0 1.9 %collective-permute-done.10 = bf16[2,2,8192]{2,1,0:T(2,128)(2,1)S(1)} collective-permute-done((bf16[2,2,8192]{2,1,0:T(2,128)(2,1)S(1)}, bf16[2,2,8192]{2,1,0:T(2,128)(2,1)S(1)}, u32[]{:S(2)}, u32[]{:S(2)}) %collective-permute-start.10) | collective-permute-done | bytes 65568 | tf_op jit(solution)/shard_map/ppermute | solution.py:570
  170.0 2.3 %collective-permute-start.11 = (bf16[1,2,8192]{2,1,0:T(2,128)(2,1)S(1)}, bf16[1,2,8192]{2,1,0:T(2,128)(2,1)S(1)}, u32[]{:S(2)}, u32[]{:S(2)}) collective-permute-start(bf16[1,2,8192]{2,1,0:T(2,128)(2,1)S(1)} %dynamic-slice_convert_fusion), channel_id=1, source_target_pairs={{0,8},{1,9},{2,10},{3,11},{4,12},{5,13},{6,14},{7,15},{8,0},{9,1},... | collective-permute-start | bytes 98312 | tf_op jit(solution)/shard_map/ppermute | solution.py:570
  172.3 2.9 %collective-permute-done.11 = bf16[1,2,8192]{2,1,0:T(2,128)(2,1)S(1)} collective-permute-done((bf16[1,2,8192]{2,1,0:T(2,128)(2,1)S(1)}, bf16[1,2,8192]{2,1,0:T(2,128)(2,1)S(1)}, u32[]{:S(2)}, u32[]{:S(2)}) %collective-permute-start.11) | collective-permute-done | bytes 32800 | tf_op jit(solution)/shard_map/ppermute | solution.py:570
  (118 shorter events, 10.4 us)
Async XLA Ops:
  1.6 16.2 %all-to-all-start = ((bf16[8,2,8192]{2,1,0:T(2,128)(2,1)}), bf16[8,2,8192]{2,1,0:T(2,128)(2,1)S(1)}, u32[]{:S(2)}, u32[]{:S(2)}) async-start(bf16[8,2,8192]{2,1,0:T(2,128)(2,1)} %broadcast_in_dim.57), calls=%async_computation | async-start | bytes 524288 | tf_op jit(solution)/shard_map/all_to_all | solution.py:530
  17.8 1.7 collective-permute-start
  24.8 12.6 %all-to-all-start.1 = ((bf16[16,32,128]{2,1,0:T(8,128)(2,1)}), bf16[16,32,128]{2,1,0:T(8,128)(2,1)S(1)}, u32[]{:S(2)}, u32[]{:S(2)}) async-start(bf16[16,32,128]{2,1,0:T(8,128)(2,1)} %broadcast_select_fusion.1), calls=%async_computation.1 | async-start | bytes 262144 | tf_op jit(solution)/shard_map/all_to_all | solution.py:530
  29.4 22.4 %copy-start = (bf16[2,64,2048]{2,1,0:T(8,128)(2,1)S(1)}, bf16[2,64,2048]{2,1,0:T(8,128)(2,1)}, u32[]{:S(2)}) copy-start(bf16[2,64,2048]{2,1,0:T(8,128)(2,1)} %cached.3) | copy-start | bytes 1572868
  29.4 22.4 %copy-start.1 = (s32[2]{0:T(128)S(1)}, s32[2]{0:T(128)}, u32[]{:S(2)}) copy-start(s32[2]{0:T(128)} %lengths.3) | copy-start | bytes 28
  70.2 1.6 collective-permute-start.1
  72.1 6.1 %collective-permute-start.4 = (bf16[68,512]{1,0:T(8,128)(2,1)S(1)}, bf16[68,512]{1,0:T(8,128)(2,1)S(1)}, u32[]{:S(2)}, u32[]{:S(2)}) collective-permute-start(bf16[68,512]{1,0:T(8,128)(2,1)S(1)} %get-tuple-element.78), channel_id=1, source_target_pairs={{0,6},{1,7},{2,4},{3,5},{4,2},{5,3},{6,0},{7,1},{8,14},{9,15},{10,... | collective-permute-start | bytes 208904 | tf_op jit(solution)/shard_map/ppermute | solution.py:570
  72.4 5.8 %collective-permute-start.3 = (bf16[68,512]{1,0:T(8,128)(2,1)S(1)}, bf16[68,512]{1,0:T(8,128)(2,1)S(1)}, u32[]{:S(2)}, u32[]{:S(2)}) collective-permute-start(bf16[68,512]{1,0:T(8,128)(2,1)S(1)} %get-tuple-element.77), channel_id=1, source_target_pairs={{0,4},{1,5},{2,6},{3,7},{4,0},{5,1},{6,2},{7,3},{8,12},{9,13},{10,... | collective-permute-start | bytes 208904 | tf_op jit(solution)/shard_map/ppermute | solution.py:570
  73.8 5.2 %collective-permute-start.2 = (bf16[68,512]{1,0:T(8,128)(2,1)S(1)}, bf16[68,512]{1,0:T(8,128)(2,1)S(1)}, u32[]{:S(2)}, u32[]{:S(2)}) collective-permute-start(bf16[68,512]{1,0:T(8,128)(2,1)S(1)} %get-tuple-element.76), channel_id=1, source_target_pairs={{0,2},{1,3},{2,0},{3,1},{4,6},{5,7},{6,4},{7,5},{8,10},{9,11},{10,... | collective-permute-start | bytes 208904 | tf_op jit(solution)/shard_map/ppermute | solution.py:570
  79.2 5.0 %collective-permute-start.5 = (bf16[36,512]{1,0:T(8,128)(2,1)S(1)}, bf16[36,512]{1,0:T(8,128)(2,1)S(1)}, u32[]{:S(2)}, u32[]{:S(2)}) collective-permute-start(bf16[36,512]{1,0:T(8,128)(2,1)S(1)} %pad_maximum_fusion.6), channel_id=1, source_target_pairs={{0,8},{1,9},{2,10},{3,11},{4,12},{5,13},{6,14},{7,15},{8,0},{9,1},... | collective-permute-start | bytes 110600 | tf_op jit(solution)/shard_map/ppermute | solution.py:570
  98.0 1.5 collective-permute-start.6
  105.0 11.4 %all-to-all-start.5 = ((bf16[16,32,128]{2,1,0:T(8,128)(2,1)}), bf16[16,32,128]{2,1,0:T(8,128)(2,1)S(1)}, u32[]{:S(2)}, u32[]{:S(2)}) async-start(bf16[16,32,128]{2,1,0:T(8,128)(2,1)} %broadcast_select_fusion), calls=%async_computation.5 | async-start | bytes 262144 | tf_op jit(solution)/shard_map/all_to_all | solution.py:530
  146.7 10.5 %all-to-all-start.8 = ((bf16[16,2,1024]{2,1,0:T(2,128)(2,1)}), bf16[16,2,1024]{2,1,0:T(2,128)(2,1)S(1)}, u32[]{:S(2)}, u32[]{:S(2)}) async-start(bf16[16,2,1024]{2,1,0:T(2,128)(2,1)} %reshape.239), calls=%async_computation.8 | async-start | bytes 131072 | tf_op jit(solution)/shard_map/all_to_all | solution.py:530
  160.9 1.6 collective-permute-start.7
  163.1 4.3 %collective-permute-start.8 = (bf16[2,2,8192]{2,1,0:T(2,128)(2,1)S(1)}, bf16[2,2,8192]{2,1,0:T(2,128)(2,1)S(1)}, u32[]{:S(2)}, u32[]{:S(2)}) collective-permute-start(bf16[2,2,8192]{2,1,0:T(2,128)(2,1)S(1)} %get-tuple-element.60), channel_id=1, source_target_pairs={{0,2},{1,3},{2,0},{3,1},{4,6},{5,7},{6,4},{7,5},{8,10},{9,11},{10,... | collective-permute-start | bytes 196616 | tf_op jit(solution)/shard_map/ppermute | solution.py:570
  163.2 4.7 %collective-permute-start.9 = (bf16[2,2,8192]{2,1,0:T(2,128)(2,1)S(1)}, bf16[2,2,8192]{2,1,0:T(2,128)(2,1)S(1)}, u32[]{:S(2)}, u32[]{:S(2)}) collective-permute-start(bf16[2,2,8192]{2,1,0:T(2,128)(2,1)S(1)} %get-tuple-element.61), channel_id=1, source_target_pairs={{0,4},{1,5},{2,6},{3,7},{4,0},{5,1},{6,2},{7,3},{8,12},{9,13},{10,... | collective-permute-start | bytes 196616 | tf_op jit(solution)/shard_map/ppermute | solution.py:570
  164.5 5.3 %collective-permute-start.10 = (bf16[2,2,8192]{2,1,0:T(2,128)(2,1)S(1)}, bf16[2,2,8192]{2,1,0:T(2,128)(2,1)S(1)}, u32[]{:S(2)}, u32[]{:S(2)}) collective-permute-start(bf16[2,2,8192]{2,1,0:T(2,128)(2,1)S(1)} %get-tuple-element.62), channel_id=1, source_target_pairs={{0,6},{1,7},{2,4},{3,5},{4,2},{5,3},{6,0},{7,1},{8,14},{9,15},{10,... | collective-permute-start | bytes 196616 | tf_op jit(solution)/shard_map/ppermute | solution.py:570
  170.0 5.2 %collective-permute-start.11 = (bf16[1,2,8192]{2,1,0:T(2,128)(2,1)S(1)}, bf16[1,2,8192]{2,1,0:T(2,128)(2,1)S(1)}, u32[]{:S(2)}, u32[]{:S(2)}) collective-permute-start(bf16[1,2,8192]{2,1,0:T(2,128)(2,1)S(1)} %dynamic-slice_convert_fusion), channel_id=1, source_target_pairs={{0,8},{1,9},{2,10},{3,11},{4,12},{5,13},{6,14},{7,15},{8,0},{9,1},... | collective-permute-start | bytes 98312 | tf_op jit(solution)/shard_map/ppermute | solution.py:570
